TPU v7x, 32 devices: a whole 2x2x4 slice. The times are simulated.
32 devices in a mesh: lat: 8 (over z, x), lon: 4 (over y, core).
Axes of the slice: x: 2, y: 2, z: 4, core: 2. Of those that a mesh axis runs over, the one named last changes fastest.
Arguments:
- grid_input: bfloat16 [8, 4, 720, 227], P('lat', 'lon'), may hold values from -6 to 6
- w_grid: bfloat16 [227, 512], replicated, may hold values from -0.375 to 0.375
- w_send: bfloat16 [512, 512], replicated, may hold values from -0.25 to 0.25
- to_sector: int32 [8, 4, 720, 1], P('lat', 'lon'), may hold values from 0 to 3; in each aligned block of 720 rows (0 to 719, 720 to 1439, ..., all dimensions but the last counted through in order) at most 360 rows name the same one
- to_node: int32 [8, 4, 720], P('lat', 'lon'), may hold values from 0 to 39
- w_node: bfloat16 [512, 512], replicated, may hold values from -0.25 to 0.25
- mesh_links: int32 [8, 4, 40, 6], P('lat', 'lon'), may hold values from 0 to 359
- w_source: bfloat16 [2, 512, 512], replicated, may hold values from -0.25 to 0.25
- w_target: bfloat16 [2, 512, 512], replicated, may hold values from -0.25 to 0.25
- w_update: bfloat16 [2, 512, 512], replicated, may hold values from -0.25 to 0.25
- w_decode: bfloat16 [512, 512], replicated, may hold values from -0.25 to 0.25
- w_output: bfloat16 [512, 227], replicated, may hold values from -0.25 to 0.25
Outputs:
- grid_output: bfloat16 [8, 4, 720, 227], P('lat', 'lon')
- mesh_state: bfloat16 [8, 4, 40, 512], P('lat', 'lon')
Inputs may be any that keep to these rules, and one draw needn't show every extreme that they name: `to_sector`: among the 720 grid points of one device, at most 360 name one sector, a bound that some block reaches.
All inputs are finite; a program needn't handle non-finite values.
Results may differ from a plain program's by a relative error of at most 0.015.
Values may be sent and summed in bfloat16 or wider, within the bound.
A program may use at most 64 MiB of HBM per device.

v0:
```python
import jax
import jax.numpy as jnp
from jax import lax
from jax.sharding import PartitionSpec as P


def extended_2(block, sides, width, periodic):
    for axis, dim in sides:
        count = lax.axis_size(axis)
        forward = [(i, i + 1) for i in range(count - 1)]
        if periodic:
            forward.append((count - 1, 0))
        backward = [(target, source) for source, target in forward]
        low = lax.ppermute(
            lax.slice_in_dim(block, block.shape[dim] - width, None, axis=dim), axis, forward
        )
        high = lax.ppermute(lax.slice_in_dim(block, 0, width, axis=dim), axis, backward)
        block = jnp.concatenate([low, block, high], axis=dim)
    return block


def layer_norm(values):
    center = values - jnp.mean(values, -1, keepdims=True)
    spread = jnp.mean(center * center, -1, keepdims=True)
    return center * lax.rsqrt(spread + 1e-05)


def matmul(left, right):
    return jnp.dot(left, right, preferred_element_type=jnp.float32)


def body(
    grid_input,
    w_grid,
    w_send,
    to_sector,
    to_node,
    w_node,
    mesh_links,
    w_source,
    w_target,
    w_update,
    w_decode,
    w_output,
):
    groups = lax.axis_size("lon")
    points = grid_input.shape[2]
    latent = w_send.shape[0]
    nodes = mesh_links.shape[2]
    hidden = jax.nn.silu(matmul(grid_input.reshape(points, -1), w_grid)).astype(jnp.bfloat16)
    message = jax.nn.silu(matmul(hidden, w_send)).astype(jnp.bfloat16)
    sector = to_sector.reshape(points)
    node_of = to_node.reshape(points)
    capacity = (2 * points + groups - 1) // groups
    chosen = (sector[:, None] == jnp.arange(groups, dtype=jnp.int32)[None, :]).astype(jnp.int32)
    before = jnp.sum((jnp.cumsum(chosen, 0) - chosen) * chosen, 1)
    position = sector * capacity + before
    buckets = jnp.zeros((groups * capacity, latent), jnp.bfloat16).at[position].set(message)
    labels = jnp.full((groups * capacity,), nodes, jnp.int32).at[position].set(node_of)
    arrived, arrived_labels = (
        lax.all_to_all(
            buckets.reshape(groups, capacity, latent),
            "lon",
            split_axis=0,
            concat_axis=0,
            tiled=True,
        ),
        lax.all_to_all(
            labels.reshape(groups, capacity), "lon", split_axis=0, concat_axis=0, tiled=True
        ),
    )
    flat_labels = arrived_labels.reshape(-1)
    selector = (
        jnp.arange(nodes, dtype=jnp.int32)[None, :, None] == arrived_labels[:, None, :]
    ).astype(jnp.bfloat16)
    partial_value = jnp.einsum(
        "gnc,gcl->gnl", selector, arrived, preferred_element_type=jnp.float32
    ).astype(jnp.bfloat16)
    gathered = jnp.sum(partial_value.astype(jnp.float32), 0)
    state = jax.nn.silu(matmul(layer_norm(gathered).astype(jnp.bfloat16), w_node)).astype(
        jnp.bfloat16
    )
    links = mesh_links.reshape(nodes, -1)
    for layer_index in range(w_source.shape[0]):
        sender = (
            matmul(state, w_source[layer_index]).astype(jnp.bfloat16).reshape(1, 1, nodes, latent)
        )
        beside = extended_2(sender, (("lon", 1),), 1, True)
        beside_all = extended_2(beside, (("lat", 0),), 1, False)
        table = beside_all.reshape(9 * nodes, latent)
        picked = table[links]
        toward = matmul(state, w_target[layer_index])
        summed = jnp.sum(jax.nn.silu(picked.astype(jnp.float32) + toward[:, None, :]), axis=1)
        lifted = layer_norm(summed).astype(jnp.bfloat16)
        state = (state.astype(jnp.float32) + matmul(lifted, w_update[layer_index])).astype(
            jnp.bfloat16
        )
    reply = jax.nn.silu(matmul(state, w_decode)).astype(jnp.bfloat16)
    extended = jnp.concatenate([reply, jnp.zeros((1, latent), jnp.bfloat16)], axis=0)
    answers = extended[flat_labels].reshape(groups, capacity, latent)
    returned = lax.all_to_all(answers, "lon", split_axis=0, concat_axis=0, tiled=True)
    fetched = returned.reshape(-1, latent)[position]
    joined = (hidden.astype(jnp.float32) + fetched.astype(jnp.float32)).astype(jnp.bfloat16)
    result = matmul(joined, w_output).astype(jnp.bfloat16)
    return (result.reshape(1, 1, points, -1), state.reshape(1, 1, nodes, latent))


def solution(mesh):
    placed = (
        P("lat", "lon", None, None),
        P(),
        P(),
        P("lat", "lon", None, None),
        P("lat", "lon", None),
        P(),
        P("lat", "lon", None, None),
        P(),
        P(),
        P(),
        P(),
        P(),
    )
    return jax.shard_map(
        body,
        mesh=mesh,
        in_specs=placed,
        out_specs=(P("lat", "lon", None, None), P("lat", "lon", None, None)),
        check_vma=False,
    )
```

profile of v0, /device:TPU:9, one launch (start us, length us, event | category | flops | bytes accessed | tf_op | source)
XLA Modules:
  0.0 114.4 jit_solution(5884606777396561979)
XLA Ops:
  2.2 1.1 %reduce-window.6 = s32[4,6,128]{2,1,0:T(8,128)S(1)} reduce-window(s32[4,6,128]{2,1,0:T(8,128)S(1)} %reshape.200, s32[]{:T(128)} %constant.38.clone.1), window={size=1x1x128 pad=0_0x0_0x127_0}, to_apply=%region_0.1 | reduce-window | flops 390144 | bytes 24580 | tf_op jit(solution)/shard_map/reduce-window
  4.5 4.1 %scatter_custom_fusion = s32[1440]{0:T(1024)S(1)} fusion(s32[720]{0:T(1024)S(1)} %fusion.41, s32[720]{0:T(1024)S(1)} %reduce.6, s32[]{:T(128)} %constant.20.clone.1), kind=kCustom, calls=%fused_computation.83 | custom fusion | bytes 5764 | tf_op jit(solution)/shard_map/scatter | solution.py:59
  9.3 3.9 %all-to-all-start = ((s32[4,1,360]{2,1,0:T(1,128)}), s32[4,1,360]{2,1,0:T(1,128)S(1)}, u32[]{:S(2)}, u32[]{:S(2)}) async-start(s32[4,1,360]{2,1,0:T(1,128)} %all_to_all.12), calls=%async_computation | async-start | bytes 12288 | tf_op jit(solution)/shard_map/all_to_all | solution.py:68
  13.2 1.6 %multiply_convert_fusion.1 = bf16[720,512]{1,0:T(8,128)(2,1)S(1)} fusion(bf16[227,512]{1,0:T(8,128)(2,1)} %param.13, bf16[1,1,720,227]{2,3,1,0:T(8,128)(2,1)} %param.12), kind=kOutput, calls=%fused_computation.8 | convolution fusion | flops 169205760 | bytes 1296608 | tf_op jit(solution)/shard_map/dot_general | solution.py:29
  15.4 7.3 %scatter_custom_fusion.1 = bf16[1440,512]{1,0:T(8,128)(2,1)} fusion(s32[720]{0:T(1024)S(1)} %fusion.41, f32[720,512]{1,0:T(8,128)S(1)} %fusion.43, bf16[]{:T(256)} %constant.40.clone.1, f32[]{:T(128)} %constant.18.clone.1), kind=kCustom, calls=%fused_computation.21 | custom fusion | flops 1843200 | bytes 2949126 | tf_op jit(solution)/shard_map/scatter | solution.py:58
  22.7 3.7 %all-to-all-start.1 = ((bf16[4,360,512]{2,1,0:T(8,128)(2,1)}), bf16[4,360,512]{2,1,0:T(8,128)(2,1)S(1)}, u32[]{:S(2)}, u32[]{:S(2)}) async-start(bf16[4,360,512]{2,1,0:T(8,128)(2,1)} %bitcast.3), calls=%async_computation.1 | async-start | bytes 2949120 | tf_op jit(solution)/shard_map/all_to_all | solution.py:61
  26.8 17.8 %all-to-all-done.1 = bf16[4,360,512]{2,1,0:T(8,128)(2,1)S(1)} async-done(((bf16[4,360,512]{2,1,0:T(8,128)(2,1)}), bf16[4,360,512]{2,1,0:T(8,128)(2,1)S(1)}, u32[]{:S(2)}, u32[]{:S(2)}) %all-to-all-start.1) | async-done | bytes 1474592 | tf_op jit(solution)/shard_map/all_to_all | solution.py:61
  47.8 2.1 %collective-permute-done.1 = bf16[1,1,40,512]{3,2,1,0:T(8,128)(2,1)S(1)} collective-permute-done((bf16[1,1,40,512]{3,2,1,0:T(8,128)(2,1)S(1)}, bf16[1,1,40,512]{3,2,1,0:T(8,128)(2,1)S(1)}, u32[]{:S(2)}, u32[]{:S(2)}) %collective-permute-start.1) | collective-permute-done | bytes 40992 | tf_op jit(solution)/shard_map/ppermute | solution.py:17
  49.9 3.0 %collective-permute-start.3 = (bf16[1,3,40,512]{3,2,1,0:T(8,128)(2,1)S(1)}, bf16[1,3,40,512]{3,2,1,0:T(8,128)(2,1)S(1)}, u32[]{:S(2)}, u32[]{:S(2)}) collective-permute-start(bf16[1,3,40,512]{3,2,1,0:T(8,128)(2,1)S(1)} %pad_maximum_fusion.2), channel_id=1, source_target_pairs={{4,0},{8,4},{12,8},{16,12},{20,16},{24,20},{28,24},{5,1},{9,5},{13... | collective-permute-start | bytes 368648 | tf_op jit(solution)/shard_map/ppermute | solution.py:17
  53.0 2.3 %collective-permute-start.2 = (bf16[1,3,40,512]{3,2,1,0:T(8,128)(2,1)S(1)}, bf16[1,3,40,512]{3,2,1,0:T(8,128)(2,1)S(1)}, u32[]{:S(2)}, u32[]{:S(2)}) collective-permute-start(bf16[1,3,40,512]{3,2,1,0:T(8,128)(2,1)S(1)} %pad_maximum_fusion.2), channel_id=1, source_target_pairs={{0,4},{4,8},{8,12},{12,16},{16,20},{20,24},{24,28},{1,5},{5,9},{9,... | collective-permute-start | bytes 368648 | tf_op jit(solution)/shard_map/ppermute | solution.py:14
  56.1 3.6 %collective-permute-done.2 = bf16[1,3,40,512]{3,2,1,0:T(8,128)(2,1)S(1)} collective-permute-done((bf16[1,3,40,512]{3,2,1,0:T(8,128)(2,1)S(1)}, bf16[1,3,40,512]{3,2,1,0:T(8,128)(2,1)S(1)}, u32[]{:S(2)}, u32[]{:S(2)}) %collective-permute-start.2) | collective-permute-done | bytes 122912 | tf_op jit(solution)/shard_map/ppermute | solution.py:14
  59.7 1.1 gather_fusion
  61.6 1.3 %fusion.2 = bf16[40,512]{1,0:T(8,128)(2,1)S(1)} fusion(bf16[2,512,512]{2,1,0:T(8,128)(2,1)} %param.21, bf16[40,512]{1,0:T(8,128)(2,1)S(1)} %multiply_convert_fusion.6, f32[40,512]{1,0:T(8,128)S(1)} %get-tuple-element.5, f32[40]{0:T(128)S(1)} %add_rsqrt_fusion.1, f32[40]{0:T(128)S(1)} %broadcast_multiply_fusion.1), kind=kOutput, calls=%fused_computation.15 | convolution fusion | flops 21094400 | bytes 688448 | tf_op jit(solution)/shard_map/dot_general | solution.py:29
  63.1 1.9 %collective-permute-start.5 = (bf16[1,1,40,512]{3,2,1,0:T(8,128)(2,1)S(1)}, bf16[1,1,40,512]{3,2,1,0:T(8,128)(2,1)S(1)}, u32[]{:S(2)}, u32[]{:S(2)}) collective-permute-start(bf16[1,1,40,512]{3,2,1,0:T(8,128)(2,1)S(1)} %fusion.5), channel_id=1, source_target_pairs={{1,0},{2,1},{3,2},{0,3},{5,4},{6,5},{7,6},{4,7},{9,8},{10,9},{11,1... | collective-permute-start | bytes 122888 | tf_op jit(solution)/shard_map/ppermute | solution.py:17
  65.7 1.6 %collective-permute-done.5 = bf16[1,1,40,512]{3,2,1,0:T(8,128)(2,1)S(1)} collective-permute-done((bf16[1,1,40,512]{3,2,1,0:T(8,128)(2,1)S(1)}, bf16[1,1,40,512]{3,2,1,0:T(8,128)(2,1)S(1)}, u32[]{:S(2)}, u32[]{:S(2)}) %collective-permute-start.5) | collective-permute-done | bytes 40992 | tf_op jit(solution)/shard_map/ppermute | solution.py:17
  67.4 3.7 %collective-permute-start.7 = (bf16[1,3,40,512]{3,2,1,0:T(8,128)(2,1)S(1)}, bf16[1,3,40,512]{3,2,1,0:T(8,128)(2,1)S(1)}, u32[]{:S(2)}, u32[]{:S(2)}) collective-permute-start(bf16[1,3,40,512]{3,2,1,0:T(8,128)(2,1)S(1)} %pad_maximum_fusion.3), channel_id=1, source_target_pairs={{4,0},{8,4},{12,8},{16,12},{20,16},{24,20},{28,24},{5,1},{9,5},{13... | collective-permute-start | bytes 368648 | tf_op jit(solution)/shard_map/ppermute | solution.py:17
  71.0 2.0 %collective-permute-start.6 = (bf16[1,3,40,512]{3,2,1,0:T(8,128)(2,1)S(1)}, bf16[1,3,40,512]{3,2,1,0:T(8,128)(2,1)S(1)}, u32[]{:S(2)}, u32[]{:S(2)}) collective-permute-start(bf16[1,3,40,512]{3,2,1,0:T(8,128)(2,1)S(1)} %pad_maximum_fusion.3), channel_id=1, source_target_pairs={{0,4},{4,8},{8,12},{12,16},{16,20},{20,24},{24,28},{1,5},{5,9},{9,... | collective-permute-start | bytes 368648 | tf_op jit(solution)/shard_map/ppermute | solution.py:14
  73.7 4.3 %collective-permute-done.6 = bf16[1,3,40,512]{3,2,1,0:T(8,128)(2,1)S(1)} collective-permute-done((bf16[1,3,40,512]{3,2,1,0:T(8,128)(2,1)S(1)}, bf16[1,3,40,512]{3,2,1,0:T(8,128)(2,1)S(1)}, u32[]{:S(2)}, u32[]{:S(2)}) %collective-permute-start.6) | collective-permute-done | bytes 122912 | tf_op jit(solution)/shard_map/ppermute | solution.py:14
  78.0 1.1 gather_fusion.1
  80.9 5.4 %gather_fusion.2 = bf16[1440,512]{1,0:T(8,128)(2,1)} fusion(bf16[41,512]{1,0:T(8,128)(2,1)S(1)} %concatenate.19, s32[2048]{0:T(1024)S(1)} %pad_clamp_fusion), kind=kCustom, calls=%fused_computation.2 | custom fusion | bytes 2954880 | tf_op jit(solution)/shard_map/gather | solution.py:100
  86.3 5.1 %all-to-all-start.2 = ((bf16[4,360,512]{2,1,0:T(8,128)(2,1)}), bf16[4,360,512]{2,1,0:T(8,128)(2,1)S(1)}, u32[]{:S(2)}, u32[]{:S(2)}) async-start(bf16[4,360,512]{2,1,0:T(8,128)(2,1)} %bitcast.15), calls=%async_computation.2 | async-start | bytes 2949120 | tf_op jit(solution)/shard_map/all_to_all | solution.py:101
  91.4 18.2 %all-to-all-done.2 = bf16[4,360,512]{2,1,0:T(8,128)(2,1)S(1)} async-done(((bf16[4,360,512]{2,1,0:T(8,128)(2,1)}), bf16[4,360,512]{2,1,0:T(8,128)(2,1)S(1)}, u32[]{:S(2)}, u32[]{:S(2)}) %all-to-all-start.2) | async-done | bytes 1474592 | tf_op jit(solution)/shard_map/all_to_all | solution.py:101
  109.5 2.8 %gather_fusion.3 = bf16[720,512]{1,0:T(8,128)(2,1)S(1)} fusion(bf16[1440,512]{1,0:T(8,128)(2,1)S(1)} %bitcast.67, s32[1024]{0:T(1024)S(1)} %pad_clamp_fusion.1), kind=kCustom, calls=%fused_computation.3 | custom fusion | bytes 1477440 | tf_op jit(solution)/shard_map/gather | solution.py:102
  112.4 2.1 %fusion = bf16[1,1,720,227]{2,3,1,0:T(8,128)(2,1)} fusion(bf16[512,227]{0,1:T(8,128)(2,1)} %param.23, bf16[720,512]{1,0:T(8,128)(2,1)S(1)} %gather_fusion.3, bf16[720,512]{1,0:T(8,128)(2,1)S(1)} %multiply_convert_fusion.1), kind=kOutput, calls=%fused_computation.10 | convolution fusion | flops 169000560 | bytes 2033888 | tf_op jit(solution)/shard_map/dot_general | solution.py:29
  (77 shorter events, 12.3 us)
Async XLA Ops:
  0.6 14.2 %copy-start = (bf16[512,512]{1,0:T(8,128)(2,1)S(1)}, bf16[512,512]{1,0:T(8,128)(2,1)}, u32[]{:S(2)}) copy-start(bf16[512,512]{1,0:T(8,128)(2,1)} %param.14) | copy-start | bytes 1572868
  9.3 13.4 %all-to-all-start = ((s32[4,1,360]{2,1,0:T(1,128)}), s32[4,1,360]{2,1,0:T(1,128)S(1)}, u32[]{:S(2)}, u32[]{:S(2)}) async-start(s32[4,1,360]{2,1,0:T(1,128)} %all_to_all.12), calls=%async_computation | async-start | bytes 12288 | tf_op jit(solution)/shard_map/all_to_all | solution.py:68
  22.7 3.7 %copy-start.7 = (s32[1,1,40,6]{2,1,3,0:T(1,128)S(1)}, s32[1,1,40,6]{2,1,3,0:T(1,128)}, u32[]{:S(2)}) copy-start(s32[1,1,40,6]{2,1,3,0:T(1,128)} %param.18) | copy-start | bytes 2884
  22.7 21.9 %all-to-all-start.1 = ((bf16[4,360,512]{2,1,0:T(8,128)(2,1)}), bf16[4,360,512]{2,1,0:T(8,128)(2,1)S(1)}, u32[]{:S(2)}, u32[]{:S(2)}) async-start(bf16[4,360,512]{2,1,0:T(8,128)(2,1)} %bitcast.3), calls=%async_computation.1 | async-start | bytes 2949120 | tf_op jit(solution)/shard_map/all_to_all | solution.py:61
  26.4 18.8 %copy-start.8 = (bf16[512,512]{1,0:T(8,128)(2,1)S(1)}, bf16[512,512]{1,0:T(8,128)(2,1)}, u32[]{:S(2)}) copy-start(bf16[512,512]{1,0:T(8,128)(2,1)} %param.17) | copy-start | bytes 1572868
  44.6 1.2 %copy-start.3 = (bf16[2,512,512]{2,1,0:T(8,128)(2,1)S(1)}, bf16[2,512,512]{2,1,0:T(8,128)(2,1)}, u32[]{:S(2)}) copy-start(bf16[2,512,512]{2,1,0:T(8,128)(2,1)} %param.19) | copy-start | bytes 3145732
  44.6 10.7 %copy-start.1 = (bf16[2,512,512]{2,1,0:T(8,128)(2,1)S(1)}, bf16[2,512,512]{2,1,0:T(8,128)(2,1)}, u32[]{:S(2)}) copy-start(bf16[2,512,512]{2,1,0:T(8,128)(2,1)} %param.20) | copy-start | bytes 3145732
  46.0 3.9 %collective-permute-start.1 = (bf16[1,1,40,512]{3,2,1,0:T(8,128)(2,1)S(1)}, bf16[1,1,40,512]{3,2,1,0:T(8,128)(2,1)S(1)}, u32[]{:S(2)}, u32[]{:S(2)}) collective-permute-start(bf16[1,1,40,512]{3,2,1,0:T(8,128)(2,1)S(1)} %fusion.4), channel_id=1, source_target_pairs={{1,0},{2,1},{3,2},{0,3},{5,4},{6,5},{7,6},{4,7},{9,8},{10,9},{11,1... | collective-permute-start | bytes 122888 | tf_op jit(solution)/shard_map/ppermute | solution.py:17
  46.9 3.0 %collective-permute-start = (bf16[1,1,40,512]{3,2,1,0:T(8,128)(2,1)S(1)}, bf16[1,1,40,512]{3,2,1,0:T(8,128)(2,1)S(1)}, u32[]{:S(2)}, u32[]{:S(2)}) collective-permute-start(bf16[1,1,40,512]{3,2,1,0:T(8,128)(2,1)S(1)} %fusion.4), channel_id=1, source_target_pairs={{0,1},{1,2},{2,3},{3,0},{4,5},{5,6},{6,7},{7,4},{8,9},{9,10},{10,1... | collective-permute-start | bytes 122888 | tf_op jit(solution)/shard_map/ppermute | solution.py:14
  49.9 6.1 %collective-permute-start.3 = (bf16[1,3,40,512]{3,2,1,0:T(8,128)(2,1)S(1)}, bf16[1,3,40,512]{3,2,1,0:T(8,128)(2,1)S(1)}, u32[]{:S(2)}, u32[]{:S(2)}) collective-permute-start(bf16[1,3,40,512]{3,2,1,0:T(8,128)(2,1)S(1)} %pad_maximum_fusion.2), channel_id=1, source_target_pairs={{4,0},{8,4},{12,8},{16,12},{20,16},{24,20},{28,24},{5,1},{9,5},{13... | collective-permute-start | bytes 368648 | tf_op jit(solution)/shard_map/ppermute | solution.py:17
  53.0 6.7 %collective-permute-start.2 = (bf16[1,3,40,512]{3,2,1,0:T(8,128)(2,1)S(1)}, bf16[1,3,40,512]{3,2,1,0:T(8,128)(2,1)S(1)}, u32[]{:S(2)}, u32[]{:S(2)}) collective-permute-start(bf16[1,3,40,512]{3,2,1,0:T(8,128)(2,1)S(1)} %pad_maximum_fusion.2), channel_id=1, source_target_pairs={{0,4},{4,8},{8,12},{12,16},{16,20},{20,24},{24,28},{1,5},{5,9},{9,... | collective-permute-start | bytes 368648 | tf_op jit(solution)/shard_map/ppermute | solution.py:14
  60.8 2.1 %copy-start.4 = (bf16[2,512,512]{2,1,0:T(8,128)(2,1)S(1)}, bf16[2,512,512]{2,1,0:T(8,128)(2,1)}, u32[]{:S(2)}) copy-start(bf16[2,512,512]{2,1,0:T(8,128)(2,1)} %param.19) | copy-start | bytes 3145732
  60.9 12.2 %copy-start.2 = (bf16[2,512,512]{2,1,0:T(8,128)(2,1)S(1)}, bf16[2,512,512]{2,1,0:T(8,128)(2,1)}, u32[]{:S(2)}) copy-start(bf16[2,512,512]{2,1,0:T(8,128)(2,1)} %param.20) | copy-start | bytes 3145732
  63.1 4.2 %collective-permute-start.5 = (bf16[1,1,40,512]{3,2,1,0:T(8,128)(2,1)S(1)}, bf16[1,1,40,512]{3,2,1,0:T(8,128)(2,1)S(1)}, u32[]{:S(2)}, u32[]{:S(2)}) collective-permute-start(bf16[1,1,40,512]{3,2,1,0:T(8,128)(2,1)S(1)} %fusion.5), channel_id=1, source_target_pairs={{1,0},{2,1},{3,2},{0,3},{5,4},{6,5},{7,6},{4,7},{9,8},{10,9},{11,1... | collective-permute-start | bytes 122888 | tf_op jit(solution)/shard_map/ppermute | solution.py:17
  65.0 2.3 %collective-permute-start.4 = (bf16[1,1,40,512]{3,2,1,0:T(8,128)(2,1)S(1)}, bf16[1,1,40,512]{3,2,1,0:T(8,128)(2,1)S(1)}, u32[]{:S(2)}, u32[]{:S(2)}) collective-permute-start(bf16[1,1,40,512]{3,2,1,0:T(8,128)(2,1)S(1)} %fusion.5), channel_id=1, source_target_pairs={{0,1},{1,2},{2,3},{3,0},{4,5},{5,6},{6,7},{7,4},{8,9},{9,10},{10,1... | collective-permute-start | bytes 122888 | tf_op jit(solution)/shard_map/ppermute | solution.py:14
  67.4 6.4 %collective-permute-start.7 = (bf16[1,3,40,512]{3,2,1,0:T(8,128)(2,1)S(1)}, bf16[1,3,40,512]{3,2,1,0:T(8,128)(2,1)S(1)}, u32[]{:S(2)}, u32[]{:S(2)}) collective-permute-start(bf16[1,3,40,512]{3,2,1,0:T(8,128)(2,1)S(1)} %pad_maximum_fusion.3), channel_id=1, source_target_pairs={{4,0},{8,4},{12,8},{16,12},{20,16},{24,20},{28,24},{5,1},{9,5},{13... | collective-permute-start | bytes 368648 | tf_op jit(solution)/shard_map/ppermute | solution.py:17
  71.0 7.0 %collective-permute-start.6 = (bf16[1,3,40,512]{3,2,1,0:T(8,128)(2,1)S(1)}, bf16[1,3,40,512]{3,2,1,0:T(8,128)(2,1)S(1)}, u32[]{:S(2)}, u32[]{:S(2)}) collective-permute-start(bf16[1,3,40,512]{3,2,1,0:T(8,128)(2,1)S(1)} %pad_maximum_fusion.3), channel_id=1, source_target_pairs={{0,4},{4,8},{8,12},{12,16},{16,20},{20,24},{24,28},{1,5},{5,9},{9,... | collective-permute-start | bytes 368648 | tf_op jit(solution)/shard_map/ppermute | solution.py:14
  79.2 1.2 %copy-start.5 = (bf16[2,512,512]{2,1,0:T(8,128)(2,1)S(1)}, bf16[2,512,512]{2,1,0:T(8,128)(2,1)}, u32[]{:S(2)}) copy-start(bf16[2,512,512]{2,1,0:T(8,128)(2,1)} %param.21) | copy-start | bytes 3145732
  79.2 1.4 %copy-start.9 = (bf16[512,512]{1,0:T(8,128)(2,1)S(1)}, bf16[512,512]{1,0:T(8,128)(2,1)}, u32[]{:S(2)}) copy-start(bf16[512,512]{1,0:T(8,128)(2,1)} %param.22) | copy-start | bytes 1572868
  80.6 5.6 %copy-start.6 = (bf16[40,512]{1,0:T(8,128)(2,1)}, bf16[40,512]{1,0:T(8,128)(2,1)S(1)}, u32[]{:S(2)}) copy-start(bf16[40,512]{1,0:T(8,128)(2,1)S(1)} %fusion.3) | copy-start | bytes 122884
  86.3 23.2 %all-to-all-start.2 = ((bf16[4,360,512]{2,1,0:T(8,128)(2,1)}), bf16[4,360,512]{2,1,0:T(8,128)(2,1)S(1)}, u32[]{:S(2)}, u32[]{:S(2)}) async-start(bf16[4,360,512]{2,1,0:T(8,128)(2,1)} %bitcast.15), calls=%async_computation.2 | async-start | bytes 2949120 | tf_op jit(solution)/shard_map/all_to_all | solution.py:101
where the time goes:
time: 115 us; the launch traced here: 114 us
  waiting for transfers between devices  48.6 us (42%)
  starting transfers between devices  28 us (24%)
  local copies, waits for them, and re-layouts  16.6 us (14%)
  other arithmetic  12.7 us (11%)
  matrix products  7.47 us (6%)
    all_to_all x1, waiting for transfers between devices, body(): lax.all_to_all(answers, 'lon', split_axis=0, concat_axis=0, tiled=True)  18.2 us
    all_to_all x1, waiting for transfers between devices, body(): lax.all_to_all(buckets.reshape(groups, capacity, latent), 'lon', split_ax...  17.8 us
    ppermute x4, starting transfers between devices, extended_2(): lax.ppermute(lax.slice_in_dim(block, 0, width, axis=dim), axis, backward)  9.51 us
    ppermute x4, waiting for transfers between devices, extended_2(): lax.ppermute(lax.slice_in_dim(block, block.shape[dim] - width, None, axis...  7.85 us
    scatter x1, other arithmetic, body(): jnp.zeros((groups * capacity, latent), jnp.bfloat16).at[position]  7.32 us
    dot_general x11, matrix products, matmul(): return jnp.dot(left, right, preferred_element_type=jnp.float32)  7.02 us
    ppermute x4, starting transfers between devices, extended_2(): lax.ppermute(lax.slice_in_dim(block, block.shape[dim] - width, None, axis...  5.85 us
    gather x1, local copies, waits for them, and re-layouts, body(): answers = extended[flat_labels].reshape(groups, capacity, latent)  5.38 us
  transfers between devices with their start and end apart: 11, of which 8 were waited for; matrix products, arithmetic and copies ran while one was open for 9% of the time, Pallas kernels for 0%

commit v1 on v0

v1 whole, which is shorter than its diff:
```python
import functools

import jax
import jax.numpy as jnp
from jax import lax
from jax.experimental import pallas as pl
from jax.experimental.pallas import tpu as pltpu
from jax.sharding import PartitionSpec as P

MESH = pl.DeviceIdType.MESH
BF16 = jnp.bfloat16


def silu(values):
    half = 0.5 * values
    return half + half * jnp.tanh(half)


def layer_norm(values):
    center = values - jnp.mean(values, -1, keepdims=True)
    spread = jnp.mean(center * center, -1, keepdims=True)
    return center * lax.rsqrt(spread + 1e-05)


def matmul(left, right, left_dim=1, right_dim=0):
    return lax.dot_general(
        left, right, (((left_dim,), (right_dim,)), ((), ())), preferred_element_type=jnp.float32
    )


def kernel(
    n_lat,
    n_lon,
    nodes,
    rows,
    chunk,
    x_hbm,
    wg_hbm,
    ws_hbm,
    sector_ref,
    node_ref,
    wn_hbm,
    links_ref,
    wsrc_hbm,
    wtgt_hbm,
    wupd_hbm,
    wdec_hbm,
    wout_hbm,
    out_ref,
    state_ref,
    x,
    wg,
    ws,
    wn,
    wsrc,
    wtgt,
    wupd,
    wdec,
    wout,
    hidden,
    message,
    part,
    part_in,
    table,
    reply_all,
    base,
    load_sem,
    part_send,
    part_recv,
    halo_send,
    halo_recv,
    reply_send,
    reply_recv,
):
    band = lax.axis_index("lat")
    sector = lax.axis_index("lon")
    points = x.shape[1]
    latent = ws.shape[0]
    layers = wsrc.shape[0]
    has_low = band > 0
    has_high = band < n_lat - 1

    loads = [
        pltpu.make_async_copy(source, target, load_sem.at[i])
        for i, (source, target) in enumerate(
            (
                (x_hbm, x),
                (wg_hbm, wg),
                (ws_hbm, ws),
                (wn_hbm, wn),
                (wsrc_hbm, wsrc),
                (wout_hbm, wout),
                (wtgt_hbm, wtgt),
                (wupd_hbm, wupd),
                (wdec_hbm, wdec),
            )
        )
    ]
    for load in loads:
        load.start()

    def beside(lat_step, lon_step):
        return (band + lat_step, lax.rem(sector + lon_step + n_lon, n_lon))

    barrier = pltpu.get_barrier_semaphore()
    for step in range(1, n_lon):
        pl.semaphore_signal(barrier, inc=1, device_id=beside(0, step), device_id_type=MESH)

    @pl.when(has_low)
    def _():
        for step in (-1, 0, 1):
            pl.semaphore_signal(barrier, inc=1, device_id=beside(-1, step), device_id_type=MESH)

    @pl.when(has_high)
    def _():
        for step in (-1, 0, 1):
            pl.semaphore_signal(barrier, inc=1, device_id=beside(1, step), device_id_type=MESH)

    zeros = jnp.zeros((3, rows, latent), BF16)

    @pl.when(band == 0)
    def _():
        for layer in range(layers):
            table[layer, 0:3] = zeros

    @pl.when(band == n_lat - 1)
    def _():
        for layer in range(layers):
            table[layer, 6:9] = zeros

    target = sector_ref[...] * rows + node_ref[...]
    total = n_lon * rows
    chosen = jnp.where(
        lax.broadcasted_iota(jnp.int32, (total, points), 0) == target, 1.0, 0.0
    ).astype(BF16)

    loads[0].wait()
    loads[1].wait()
    hidden[...] = silu(matmul(x[...], wg[...], 0, 0)).astype(BF16)
    loads[2].wait()
    for start in range(0, points, chunk):
        span = pl.ds(start, chunk)
        message[span, :] = silu(matmul(hidden[span, :], ws[...])).astype(BF16)
    part[...] = matmul(chosen, message[...]).astype(BF16).reshape(n_lon, rows, latent)

    inner = jnp.logical_and(has_low, has_high)

    @pl.when(inner)
    def _():
        pl.semaphore_wait(barrier, n_lon - 1 + 6)

    @pl.when(jnp.logical_not(inner))
    def _():
        pl.semaphore_wait(barrier, n_lon - 1 + 3)

    sends = []
    for step in range(1, n_lon):
        copy = pltpu.make_async_remote_copy(
            src_ref=part.at[lax.rem(sector + step, n_lon)],
            dst_ref=part_in.at[step - 1],
            send_sem=part_send.at[step - 1],
            recv_sem=part_recv.at[step - 1],
            device_id=beside(0, step),
            device_id_type=MESH,
        )
        copy.start()
        sends.append(copy)

    loads[5].wait()
    base[...] = matmul(wout[...], hidden[...], 1, 1)
    links = links_ref[...]
    links = links + (rows - nodes) * (links // nodes)
    degree = links.shape[0]
    links = jnp.swapaxes(links, 0, 1)
    filler = jnp.zeros((rows - nodes, 1), jnp.int32)
    pieces = []
    for k in range(degree):
        pieces += [links[:, k : k + 1], filler]
    links = jnp.concatenate(pieces, axis=0)
    wanted = jnp.where(
        lax.broadcasted_iota(jnp.int32, (degree * rows, 9 * rows), 1) == links, 1.0, 0.0
    ).astype(BF16)

    gathered = part[sector].astype(jnp.float32)
    loads[3].wait()
    for step in range(1, n_lon):
        sends[step - 1].wait_recv()
        gathered = gathered + part_in[step - 1].astype(jnp.float32)
    state = silu(matmul(layer_norm(gathered).astype(BF16), wn[...])).astype(BF16)

    def halo(layer, lat_step, lon_step):
        slot = (1 - lat_step) * 3 + (1 - lon_step)
        return pltpu.make_async_remote_copy(
            src_ref=table.at[layer, 4],
            dst_ref=table.at[layer, slot],
            send_sem=halo_send.at[layer, slot],
            recv_sem=halo_recv.at[layer, slot],
            device_id=beside(lat_step, lon_step),
            device_id_type=MESH,
        )

    loads[4].wait()
    for layer in range(layers):
        table[layer, 4] = matmul(state, wsrc[layer]).astype(BF16)

        @pl.when(has_low)
        def _():
            for lon_step in (-1, 0, 1):
                halo(layer, -1, lon_step).start()

        @pl.when(has_high)
        def _():
            for lon_step in (-1, 0, 1):
                halo(layer, 1, lon_step).start()

        for lon_step in (-1, 1):
            halo(layer, 0, lon_step).start()
        if layer == 0:
            loads[6].wait()
            loads[7].wait()
        toward = matmul(state, wtgt[layer])
        for lon_step in (-1, 1):
            halo(layer, 0, lon_step).wait_recv()

        @pl.when(has_low)
        def _():
            for lon_step in (-1, 0, 1):
                halo(layer, 1, lon_step).wait_recv()

        @pl.when(has_high)
        def _():
            for lon_step in (-1, 0, 1):
                halo(layer, -1, lon_step).wait_recv()

        picked = matmul(wanted, table[layer].reshape(9 * rows, latent))
        summed = silu(picked[0:rows] + toward)
        for k in range(1, degree):
            summed = summed + silu(picked[k * rows : (k + 1) * rows] + toward)
        lifted = layer_norm(summed).astype(BF16)
        state = (state.astype(jnp.float32) + matmul(lifted, wupd[layer])).astype(BF16)

    loads[8].wait()
    reply = silu(matmul(state, wdec[...])).astype(BF16)
    reply_all[sector] = matmul(reply, wout[...], 1, 1).astype(BF16)
    replies = []
    for step in range(1, n_lon):
        copy = pltpu.make_async_remote_copy(
            src_ref=reply_all.at[sector],
            dst_ref=reply_all.at[sector],
            send_sem=reply_send.at[step - 1],
            recv_sem=reply_recv.at[step - 1],
            device_id=beside(0, step),
            device_id_type=MESH,
        )
        copy.start()
        replies.append(copy)
    state_ref[...] = state[0:nodes]
    for copy in sends:
        copy.wait_send()
    for layer in range(layers):
        for lon_step in (-1, 1):
            halo(layer, 0, lon_step).wait_send()

        @pl.when(has_low)
        def _():
            for lon_step in (-1, 0, 1):
                halo(layer, -1, lon_step).wait_send()

        @pl.when(has_high)
        def _():
            for lon_step in (-1, 0, 1):
                halo(layer, 1, lon_step).wait_send()

    for step in range(1, n_lon):
        source = lax.rem(sector - step + n_lon, n_lon)
        pltpu.make_async_remote_copy(
            src_ref=reply_all.at[source],
            dst_ref=reply_all.at[source],
            send_sem=reply_send.at[step - 1],
            recv_sem=reply_recv.at[step - 1],
            device_id=beside(0, step),
            device_id_type=MESH,
        ).wait_recv()
    fetched = matmul(reply_all[...].reshape(total, -1), chosen, 0, 0)
    out_ref[...] = (base[...] + fetched).astype(BF16)
    for copy in replies:
        copy.wait_send()


def body(
    grid_input,
    w_grid,
    w_send,
    to_sector,
    to_node,
    w_node,
    mesh_links,
    w_source,
    w_target,
    w_update,
    w_decode,
    w_output,
):
    n_lat = lax.axis_size("lat")
    n_lon = lax.axis_size("lon")
    points, variables = grid_input.shape[2:]
    latent = w_send.shape[0]
    nodes = mesh_links.shape[2]
    layers = w_source.shape[0]
    rows = -(-nodes // 16) * 16
    chunk = points // 3 if points % 48 == 0 else points
    hbm = pl.BlockSpec(memory_space=pltpu.HBM)
    vmem = pl.BlockSpec(memory_space=pltpu.VMEM)
    square = pltpu.VMEM((latent, latent), BF16)
    cube = pltpu.VMEM((layers, latent, latent), BF16)
    result, state = pl.pallas_call(
        functools.partial(kernel, n_lat, n_lon, nodes, rows, chunk),
        out_shape=(
            jax.ShapeDtypeStruct((variables, points), BF16),
            jax.ShapeDtypeStruct((nodes, latent), BF16),
        ),
        in_specs=[hbm, hbm, hbm, vmem, vmem, hbm, vmem, hbm, hbm, hbm, hbm, hbm],
        out_specs=(vmem, vmem),
        scratch_shapes=[
            pltpu.VMEM((variables, points), BF16),
            pltpu.VMEM((variables, latent), BF16),
            square,
            square,
            cube,
            cube,
            cube,
            square,
            pltpu.VMEM((variables, latent), BF16),
            pltpu.VMEM((points, latent), BF16),
            pltpu.VMEM((points, latent), BF16),
            pltpu.VMEM((n_lon, rows, latent), BF16),
            pltpu.VMEM((n_lon - 1, rows, latent), BF16),
            pltpu.VMEM((layers, 9, rows, latent), BF16),
            pltpu.VMEM((n_lon, rows, variables), BF16),
            pltpu.VMEM((variables, points), jnp.float32),
            pltpu.SemaphoreType.DMA((9,)),
            pltpu.SemaphoreType.DMA((n_lon - 1,)),
            pltpu.SemaphoreType.DMA((n_lon - 1,)),
            pltpu.SemaphoreType.DMA((layers, 9)),
            pltpu.SemaphoreType.DMA((layers, 9)),
            pltpu.SemaphoreType.DMA((n_lon - 1,)),
            pltpu.SemaphoreType.DMA((n_lon - 1,)),
        ],
        compiler_params=pltpu.CompilerParams(
            collective_id=0, has_side_effects=True, vmem_limit_bytes=40 * 1024 * 1024
        ),
    )(
        jnp.swapaxes(grid_input.reshape(points, variables), 0, 1),
        w_grid,
        w_send,
        to_sector.reshape(1, points),
        to_node.reshape(1, points),
        w_node,
        jnp.swapaxes(mesh_links.reshape(nodes, -1), 0, 1),
        w_source,
        w_target,
        w_update,
        w_decode,
        jnp.swapaxes(w_output, 0, 1),
    )
    return (jnp.swapaxes(result, 0, 1).reshape(1, 1, points, variables), state.reshape(1, 1, nodes, latent))


def solution(mesh):
    placed = (
        P("lat", "lon", None, None),
        P(),
        P(),
        P("lat", "lon", None, None),
        P("lat", "lon", None),
        P(),
        P("lat", "lon", None, None),
        P(),
        P(),
        P(),
        P(),
        P(),
    )
    return jax.shard_map(
        body,
        mesh=mesh,
        in_specs=placed,
        out_specs=(P("lat", "lon", None, None), P("lat", "lon", None, None)),
        check_vma=False,
    )
```

time: 115 us -> 43.9 us (0.38)
  waiting for transfers between devices: 48.6 us -> 0 us
  Pallas kernels: 0 us -> 30.3 us
  starting transfers between devices: 28 us -> 0 us
  other arithmetic: 12.7 us -> 0 us
  matrix products: 7.47 us -> 0 us
  local copies, waits for them, and re-layouts: 16.6 us -> 12.4 us
    all_to_all x3 -> x0, waiting for transfers between devices: 35.9 us -> none  [the longest x1 18.2 us: body(): lax.all_to_all(answers, 'lon', split_axis=0, concat_axis=0, tiled=True)]
    pallas_call x0 -> x1, Pallas kernels: none -> 30.3 us  [body(): pl.pallas_call(functools.partial(kernel, n_lat, n_lon, nodes, rows, chunk...]
    ppermute x8 -> x0, starting transfers between devices: 15.4 us -> none  [the longest x4 9.51 us: extended_2(): lax.ppermute(lax.slice_in_dim(block, 0, width, axis=dim), axis, backward)]
    ppermute x8 -> x0, waiting for transfers between devices: 12.7 us -> none  [the longest x4 7.85 us: extended_2(): lax.ppermute(lax.slice_in_dim(block, block.shape[dim] - width, None, axis...]
    all_to_all x3 -> x0, starting transfers between devices: 12.7 us -> none  [the longest x1 5.07 us: body(): lax.all_to_all(answers, 'lon', split_axis=0, concat_axis=0, tiled=True)]
    unnamed x22 -> x27, local copies, waits for them, and re-layouts: 0.78 us -> 12.4 us
    gather x4 -> x0, local copies, waits for them, and re-layouts: 10.4 us -> none  [the longest x1 5.38 us: body(): answers = extended[flat_labels].reshape(groups, capacity, latent)]
    dot_general x12 -> x0, matrix products: 7.47 us -> none  [the longest x11 7.02 us: matmul(): return jnp.dot(left, right, preferred_element_type=jnp.float32)]
  transfers between devices with their start and end apart: 11 -> 0, of which waited for: 8 -> 0; matrix products, arithmetic and copies ran while one was open for 9% -> 0% of each run, Pallas kernels for 0% -> 0%
where the time goes in v1:
time: 43.9 us; the launch traced here: 43.4 us
  Pallas kernels  30.3 us (69%)
  local copies, waits for them, and re-layouts  12.4 us (28%)
  between operations  0.66 us (2%)
    pallas_call x1, Pallas kernels, body(): pl.pallas_call(functools.partial(kernel, n_lat, n_lon, nodes, rows, chunk...  30.3 us
    unnamed x27, local copies, waits for them, and re-layouts  12.4 us

profile of v1, /device:TPU:9, one launch (start us, length us, event | category | flops | bytes accessed | tf_op | source)
XLA Modules:
  0.0 43.4 jit_solution(9766846229826200566)
XLA Ops:
  0.6 0.0 copy-start.11
  0.6 0.7 %copy-done.11 = s32[1,1,40,6]{2,1,3,0:T(1,128)S(1)} copy-done((s32[1,1,40,6]{2,1,3,0:T(1,128)S(1)}, s32[1,1,40,6]{2,1,3,0:T(1,128)}, u32[]{:S(2)}) %copy-start.11) | copy-done | bytes 984
  1.3 0.0 copy-start.9
  1.3 0.0 copy-start.10
  1.3 0.7 %copy-done.9 = s32[1,1,720,1]{2,3,1,0:T(1,128)S(1)} copy-done((s32[1,1,720,1]{2,3,1,0:T(1,128)S(1)}, s32[1,1,720,1]{2,3,1,0:T(1,128)}, u32[]{:S(2)}) %copy-start.9) | copy-done | bytes 2904
  2.0 0.0 copy-done.10
  2.0 0.0 copy-start
  2.0 1.2 %copy-done = bf16[2,512,512]{2,1,0:T(8,128)(2,1)S(1)} copy-done((bf16[2,512,512]{2,1,0:T(8,128)(2,1)S(1)}, bf16[2,512,512]{2,1,0:T(8,128)(2,1)}, u32[]{:S(2)}) %copy-start) | copy-done | bytes 1048600
  3.2 0.0 copy-start.1
  3.2 1.2 %copy-done.1 = bf16[2,512,512]{2,1,0:T(8,128)(2,1)S(1)} copy-done((bf16[2,512,512]{2,1,0:T(8,128)(2,1)S(1)}, bf16[2,512,512]{2,1,0:T(8,128)(2,1)}, u32[]{:S(2)}) %copy-start.1) | copy-done | bytes 1048600
  4.5 0.0 copy-start.2
  4.5 1.2 %copy-done.2 = bf16[2,512,512]{2,1,0:T(8,128)(2,1)S(1)} copy-done((bf16[2,512,512]{2,1,0:T(8,128)(2,1)S(1)}, bf16[2,512,512]{2,1,0:T(8,128)(2,1)}, u32[]{:S(2)}) %copy-start.2) | copy-done | bytes 1048600
  5.7 0.0 copy-start.3
  5.7 1.0 %copy-done.3 = bf16[512,512]{1,0:T(8,128)(2,1)S(1)} copy-done((bf16[512,512]{1,0:T(8,128)(2,1)S(1)}, bf16[512,512]{1,0:T(8,128)(2,1)}, u32[]{:S(2)}) %copy-start.3) | copy-done | bytes 524312
  6.7 1.0 %copy-done.4 = bf16[512,512]{1,0:T(8,128)(2,1)S(1)} copy-done((bf16[512,512]{1,0:T(8,128)(2,1)S(1)}, bf16[512,512]{1,0:T(8,128)(2,1)}, u32[]{:S(2)}) %copy-start.4) | copy-done | bytes 524312
  7.8 0.0 copy-start.5
  7.8 1.0 %copy-done.5 = bf16[512,512]{1,0:T(8,128)(2,1)S(1)} copy-done((bf16[512,512]{1,0:T(8,128)(2,1)S(1)}, bf16[512,512]{1,0:T(8,128)(2,1)}, u32[]{:S(2)}) %copy-start.5) | copy-done | bytes 524312
  8.8 0.0 copy-start.6
  8.8 1.0 %copy-done.6 = bf16[1,1,720,227]{2,3,1,0:T(8,128)(2,1)S(1)} copy-done((bf16[1,1,720,227]{2,3,1,0:T(8,128)(2,1)S(1)}, bf16[1,1,720,227]{2,3,1,0:T(8,128)(2,1)}, u32[]{:S(2)}) %copy-start.6) | copy-done | bytes 326904
  9.8 0.9 %copy-done.7 = bf16[227,512]{1,0:T(8,128)(2,1)S(1)} copy-done((bf16[227,512]{1,0:T(8,128)(2,1)S(1)}, bf16[227,512]{1,0:T(8,128)(2,1)}, u32[]{:S(2)}) %copy-start.7) | copy-done | bytes 232472
  10.7 0.9 %copy-done.8 = bf16[512,227]{0,1:T(8,128)(2,1)S(1)} copy-done((bf16[512,227]{0,1:T(8,128)(2,1)S(1)}, bf16[512,227]{0,1:T(8,128)(2,1)}, u32[]{:S(2)}) %copy-start.8) | copy-done | bytes 232472
  11.7 30.3 %shard_map.131 = (bf16[227,720]{1,0:T(8,128)(2,1)S(1)}, bf16[40,512]{1,0:T(8,128)(2,1)S(1)}) custom-call(bf16[227,720]{1,0:T(8,128)(2,1)S(1)} %bitcast.16, bf16[227,512]{1,0:T(8,128)(2,1)S(1)} %copy-done.7, bf16[512,512]{1,0:T(8,128)(2,1)S(1)} %copy-done.3, s32[1,720]{1,0:T(1,128)S(1)} %bitcast.20, s32[1,720]{1,0:T(1,128)S(1)} %bitcast.21, ...), custom_call_target="tpu_custom_call" | custom-call | tf_op jit(solution)/shard_map/pallas_call | solution.py:316
  42.0 0.7 %copy.19 = bf16[1,1,720,227]{2,3,1,0:T(8,128)(2,1)} copy(bf16[1,1,720,227]{2,3,1,0:T(8,128)(2,1)S(1)} %bitcast.15) | data formatting | bytes 653760
  42.7 0.6 %copy.20 = bf16[1,1,40,512]{3,2,1,0:T(8,128)(2,1)} copy(bf16[1,1,40,512]{3,2,1,0:T(8,128)(2,1)S(1)} %bitcast.18) | data formatting | bytes 81920
  (4 shorter events, 0.0 us)
Async XLA Ops:
  0.6 0.7 %copy-start.11 = (s32[1,1,40,6]{2,1,3,0:T(1,128)S(1)}, s32[1,1,40,6]{2,1,3,0:T(1,128)}, u32[]{:S(2)}) copy-start(s32[1,1,40,6]{2,1,3,0:T(1,128)} %param.18) | copy-start | bytes 2884
  1.3 0.7 %copy-start.9 = (s32[1,1,720,1]{2,3,1,0:T(1,128)S(1)}, s32[1,1,720,1]{2,3,1,0:T(1,128)}, u32[]{:S(2)}) copy-start(s32[1,1,720,1]{2,3,1,0:T(1,128)} %param.15) | copy-start | bytes 8644
  1.3 0.7 %copy-start.10 = (s32[1,1,720]{2,1,0:T(1,128)S(1)}, s32[1,1,720]{2,1,0:T(1,128)}, u32[]{:S(2)}) copy-start(s32[1,1,720]{2,1,0:T(1,128)} %param.16) | copy-start | bytes 8644
  2.0 1.2 %copy-start = (bf16[2,512,512]{2,1,0:T(8,128)(2,1)S(1)}, bf16[2,512,512]{2,1,0:T(8,128)(2,1)}, u32[]{:S(2)}) copy-start(bf16[2,512,512]{2,1,0:T(8,128)(2,1)} %wsrc_hbm.1) | copy-start | bytes 3145732
  3.2 1.2 %copy-start.1 = (bf16[2,512,512]{2,1,0:T(8,128)(2,1)S(1)}, bf16[2,512,512]{2,1,0:T(8,128)(2,1)}, u32[]{:S(2)}) copy-start(bf16[2,512,512]{2,1,0:T(8,128)(2,1)} %wtgt_hbm.1) | copy-start | bytes 3145732
  4.5 1.2 %copy-start.2 = (bf16[2,512,512]{2,1,0:T(8,128)(2,1)S(1)}, bf16[2,512,512]{2,1,0:T(8,128)(2,1)}, u32[]{:S(2)}) copy-start(bf16[2,512,512]{2,1,0:T(8,128)(2,1)} %wupd_hbm.1) | copy-start | bytes 3145732
  5.7 1.0 %copy-start.3 = (bf16[512,512]{1,0:T(8,128)(2,1)S(1)}, bf16[512,512]{1,0:T(8,128)(2,1)}, u32[]{:S(2)}) copy-start(bf16[512,512]{1,0:T(8,128)(2,1)} %ws_hbm.1) | copy-start | bytes 1572868
  6.7 1.0 %copy-start.4 = (bf16[512,512]{1,0:T(8,128)(2,1)S(1)}, bf16[512,512]{1,0:T(8,128)(2,1)}, u32[]{:S(2)}) copy-start(bf16[512,512]{1,0:T(8,128)(2,1)} %wn_hbm.1) | copy-start | bytes 1572868
  7.8 1.0 %copy-start.5 = (bf16[512,512]{1,0:T(8,128)(2,1)S(1)}, bf16[512,512]{1,0:T(8,128)(2,1)}, u32[]{:S(2)}) copy-start(bf16[512,512]{1,0:T(8,128)(2,1)} %wdec_hbm.1) | copy-start | bytes 1572868
  8.8 1.0 %copy-start.6 = (bf16[1,1,720,227]{2,3,1,0:T(8,128)(2,1)S(1)}, bf16[1,1,720,227]{2,3,1,0:T(8,128)(2,1)}, u32[]{:S(2)}) copy-start(bf16[1,1,720,227]{2,3,1,0:T(8,128)(2,1)} %param.12) | copy-start | bytes 980644
  9.8 0.9 %copy-start.7 = (bf16[227,512]{1,0:T(8,128)(2,1)S(1)}, bf16[227,512]{1,0:T(8,128)(2,1)}, u32[]{:S(2)}) copy-start(bf16[227,512]{1,0:T(8,128)(2,1)} %wg_hbm.1) | copy-start | bytes 697348
  10.7 0.9 %copy-start.8 = (bf16[512,227]{0,1:T(8,128)(2,1)S(1)}, bf16[512,227]{0,1:T(8,128)(2,1)}, u32[]{:S(2)}) copy-start(bf16[512,227]{0,1:T(8,128)(2,1)} %param.23) | copy-start | bytes 697348

commit v2 on v1

v2 whole, which is shorter than its diff:
```python
import functools

import jax
import jax.numpy as jnp
from jax import lax
from jax.experimental import pallas as pl
from jax.experimental.pallas import tpu as pltpu
from jax.sharding import PartitionSpec as P

MESH = pl.DeviceIdType.MESH
BF16 = jnp.bfloat16
RELAYED = ()
LIMIT = 56


def silu(values):
    half = 0.5 * values
    return half + half * jnp.tanh(half)


def layer_norm(values):
    center = values - jnp.mean(values, -1, keepdims=True)
    spread = jnp.mean(center * center, -1, keepdims=True)
    return center * lax.rsqrt(spread + 1e-05)


def matmul(left, right, left_dim=1, right_dim=0):
    return lax.dot_general(
        left, right, (((left_dim,), (right_dim,)), ((), ())), preferred_element_type=jnp.float32
    )


def kernel(
    n_lat,
    n_lon,
    relayed,
    chunk,
    x_hbm,
    wg_hbm,
    ws_hbm,
    sector_hbm,
    node_hbm,
    wn_hbm,
    links_hbm,
    wsrc_hbm,
    wtgt_hbm,
    wupd_hbm,
    wdec_hbm,
    wout_hbm,
    out_ref,
    state_ref,
    x,
    wg,
    ws,
    sector_of,
    node_of,
    wn,
    links_of,
    wsrc,
    wtgt,
    wupd,
    wdec,
    wout,
    hidden,
    message,
    part,
    part_in,
    table,
    reply_all,
    base,
    load_sem,
    part_send,
    part_recv,
    halo_send,
    halo_recv,
    reply_send,
    reply_recv,
):
    band = lax.axis_index("lat")
    sector = lax.axis_index("lon")
    points = x.shape[1]
    latent = ws.shape[0]
    half = latent // 2
    layers = wsrc.shape[0]
    nodes = state_ref.shape[0]
    rows = reply_all.shape[1]
    has_low = band > 0
    has_high = band < n_lat - 1
    side = 1 - 2 * lax.rem(sector, 2)
    columns = (0, side, -side)

    loads = [
        pltpu.make_async_copy(source, target, load_sem.at[i])
        for i, (source, target) in enumerate(
            (
                (x_hbm, x),
                (wg_hbm, wg),
                (ws_hbm, ws),
                (sector_hbm, sector_of),
                (node_hbm, node_of),
                (links_hbm, links_of),
                (wout_hbm, wout),
                (wn_hbm, wn),
                (wsrc_hbm, wsrc),
                (wtgt_hbm, wtgt),
                (wupd_hbm, wupd),
                (wdec_hbm, wdec),
            )
        )
    ]
    for load in loads:
        load.start()

    def beside(lat_step, lon_step):
        return (band + lat_step, lax.rem(sector + lon_step + n_lon, n_lon))

    direct = [column for column in (0, 2, 1) if column not in relayed]
    barrier = pltpu.get_barrier_semaphore()
    for step in range(1, n_lon):
        pl.semaphore_signal(barrier, inc=1, device_id=beside(0, step), device_id_type=MESH)

    @pl.when(has_low)
    def _():
        for column in direct:
            pl.semaphore_signal(
                barrier, inc=1, device_id=beside(-1, columns[column]), device_id_type=MESH
            )

    @pl.when(has_high)
    def _():
        for column in direct:
            pl.semaphore_signal(
                barrier, inc=1, device_id=beside(1, columns[column]), device_id_type=MESH
            )

    zeros = jnp.zeros((3, 2 * nodes, half), BF16)

    @pl.when(band == 0)
    def _():
        for layer in range(layers):
            table[layer, 0:3] = zeros

    @pl.when(band == n_lat - 1)
    def _():
        for layer in range(layers):
            table[layer, 6:9] = zeros

    loads[0].wait()
    loads[1].wait()
    hidden[...] = silu(matmul(x[...], wg[...], 0, 0)).astype(BF16)
    loads[2].wait()
    for start in range(0, points, chunk):
        span = pl.ds(start, chunk)
        message[span, :] = silu(matmul(hidden[span, :], ws[...])).astype(BF16)
    loads[3].wait()
    loads[4].wait()
    target = sector_of[...] * nodes + node_of[...]
    chosen = jnp.where(
        lax.broadcasted_iota(jnp.int32, (n_lon * nodes, points), 0) == target, 1.0, 0.0
    ).astype(BF16)
    partial = matmul(chosen, message[...])
    for other in range(n_lon):
        block = partial[other * nodes : (other + 1) * nodes]
        part[other] = jnp.concatenate([block[:, :half], block[:, half:]], axis=0).astype(BF16)

    inner = jnp.logical_and(has_low, has_high)

    @pl.when(inner)
    def _():
        pl.semaphore_wait(barrier, n_lon - 1 + 2 * len(direct))

    @pl.when(jnp.logical_not(inner))
    def _():
        pl.semaphore_wait(barrier, n_lon - 1 + len(direct))

    sends = []
    for step in range(1, n_lon):
        copy = pltpu.make_async_remote_copy(
            src_ref=part.at[lax.rem(sector + step, n_lon)],
            dst_ref=part_in.at[step - 1],
            send_sem=part_send.at[step - 1],
            recv_sem=part_recv.at[step - 1],
            device_id=beside(0, step),
            device_id_type=MESH,
        )
        copy.start()
        sends.append(copy)

    loads[5].wait()
    loads[6].wait()
    base[...] = matmul(wout[...], hidden[...], 1, 1)
    degree = links_of.shape[0]
    links = jnp.swapaxes(jnp.concatenate([links_of[k] for k in range(degree)], axis=0), 0, 1)
    links = jnp.concatenate([links[:, k : k + 1] for k in range(degree)], axis=0)
    cell = links // nodes
    lon_step = cell % 3 - 1
    column = jnp.where(lon_step == 0, 0, jnp.where(lon_step == side, 1, 2))
    links = links - cell * nodes + ((cell // 3) * 3 + column) * (2 * nodes)
    slots = lax.broadcasted_iota(jnp.int32, (degree * nodes, 18 * nodes), 1)
    wanted_low = jnp.where(slots == links, 1.0, 0.0).astype(BF16)
    wanted_high = jnp.where(slots == links + nodes, 1.0, 0.0).astype(BF16)
    answered = sector_of[...] * rows + node_of[...]
    fetching = jnp.where(
        lax.broadcasted_iota(jnp.int32, (n_lon * rows, points), 0) == answered, 1.0, 0.0
    ).astype(BF16)

    gathered = part[sector].astype(jnp.float32)
    for load in loads[7:]:
        load.wait()
    for step in range(1, n_lon):
        sends[step - 1].wait_recv()
        gathered = gathered + part_in[step - 1].astype(jnp.float32)
    gathered = jnp.concatenate([gathered[:nodes], gathered[nodes:]], axis=1)
    state = silu(matmul(layer_norm(gathered).astype(BF16), wn[...])).astype(BF16)

    def halo(layer, lat_step, column, source=3):
        slot = (1 - lat_step) * 3 + column
        return pltpu.make_async_remote_copy(
            src_ref=table.at[layer, source],
            dst_ref=table.at[layer, slot],
            send_sem=halo_send.at[layer, slot],
            recv_sem=halo_recv.at[layer, slot],
            device_id=beside(lat_step, columns[column]),
            device_id_type=MESH,
        )

    def forward(layer, row, column):
        slot = row * 3 + column
        return pltpu.make_async_remote_copy(
            src_ref=table.at[layer, row * 3],
            dst_ref=table.at[layer, slot],
            send_sem=halo_send.at[layer, slot],
            recv_sem=halo_recv.at[layer, slot],
            device_id=beside(0, columns[column]),
            device_id_type=MESH,
        )

    for layer in range(layers):
        own = matmul(state, wsrc[layer])
        table[layer, 3] = jnp.concatenate([own[:, :half], own[:, half:]], axis=0).astype(BF16)

        @pl.when(has_high)
        def _():
            for column in direct:
                halo(layer, 1, column).start()

        @pl.when(has_low)
        def _():
            for column in direct:
                halo(layer, -1, column).start()

        for column in (2, 1):
            halo(layer, 0, column).start()
        toward = matmul(state, wtgt[layer])

        @pl.when(has_low)
        def _():
            halo(layer, 1, 0).wait_recv()
            for column in relayed:
                forward(layer, 0, column).start()

        @pl.when(has_high)
        def _():
            halo(layer, -1, 0).wait_recv()
            for column in relayed:
                forward(layer, 2, column).start()

        for column in (1, 2):
            halo(layer, 0, column).wait_recv()

        @pl.when(has_low)
        def _():
            for column in (2, 1):
                halo(layer, 1, column).wait_recv()

        @pl.when(has_high)
        def _():
            for column in (2, 1):
                halo(layer, -1, column).wait_recv()

        senders = table[layer].reshape(18 * nodes, half)
        picked = jnp.concatenate(
            [matmul(wanted_low, senders), matmul(wanted_high, senders)], axis=1
        )
        summed = silu(picked[0:nodes] + toward)
        for k in range(1, degree):
            summed = summed + silu(picked[k * nodes : (k + 1) * nodes] + toward)
        lifted = layer_norm(summed).astype(BF16)
        state = (state.astype(jnp.float32) + matmul(lifted, wupd[layer])).astype(BF16)

    reply = silu(matmul(state, wdec[...])).astype(BF16)
    reply = matmul(reply, wout[...], 1, 1)
    if rows > nodes:
        filler = jnp.zeros((rows - nodes, reply.shape[1]), jnp.float32)
        reply = jnp.concatenate([reply, filler], axis=0)
    reply_all[sector] = reply.astype(BF16)
    replies = []
    for step in range(1, n_lon):
        copy = pltpu.make_async_remote_copy(
            src_ref=reply_all.at[sector],
            dst_ref=reply_all.at[sector],
            send_sem=reply_send.at[step - 1],
            recv_sem=reply_recv.at[step - 1],
            device_id=beside(0, step),
            device_id_type=MESH,
        )
        copy.start()
        replies.append(copy)
    state_ref[...] = state
    for copy in sends:
        copy.wait_send()
    for layer in range(layers):
        for column in (1, 2):
            halo(layer, 0, column).wait_send()

        @pl.when(has_low)
        def _():
            for column in direct:
                halo(layer, -1, column).wait_send()
            for column in relayed:
                forward(layer, 0, column).wait_send()

        @pl.when(has_high)
        def _():
            for column in direct:
                halo(layer, 1, column).wait_send()
            for column in relayed:
                forward(layer, 2, column).wait_send()

    for step in range(1, n_lon):
        source = lax.rem(sector - step + n_lon, n_lon)
        pltpu.make_async_remote_copy(
            src_ref=reply_all.at[source],
            dst_ref=reply_all.at[source],
            send_sem=reply_send.at[step - 1],
            recv_sem=reply_recv.at[step - 1],
            device_id=beside(0, step),
            device_id_type=MESH,
        ).wait_recv()
    fetched = matmul(reply_all[...].reshape(n_lon * rows, -1), fetching, 0, 0)
    out_ref[...] = (base[...] + fetched).astype(BF16)
    for copy in replies:
        copy.wait_send()


def body(
    grid_input,
    w_grid,
    w_send,
    to_sector,
    to_node,
    w_node,
    mesh_links,
    w_source,
    w_target,
    w_update,
    w_decode,
    w_output,
):
    n_lat = lax.axis_size("lat")
    n_lon = lax.axis_size("lon")
    points, variables = grid_input.shape[2:]
    latent = w_send.shape[0]
    nodes = mesh_links.shape[2]
    layers = w_source.shape[0]
    rows = -(-nodes // 16) * 16
    chunk = points // 3 if points % 48 == 0 else points
    hbm = pl.BlockSpec(memory_space=pltpu.HBM)
    vmem = pl.BlockSpec(memory_space=pltpu.VMEM)
    square = pltpu.VMEM((latent, latent), BF16)
    cube = pltpu.VMEM((layers, latent, latent), BF16)
    result, state = pl.pallas_call(
        functools.partial(kernel, n_lat, n_lon, RELAYED, chunk),
        out_shape=(
            jax.ShapeDtypeStruct((variables, points), BF16),
            jax.ShapeDtypeStruct((nodes, latent), BF16),
        ),
        in_specs=[hbm] * 12,
        out_specs=(vmem, vmem),
        scratch_shapes=[
            pltpu.VMEM((variables, points), BF16),
            pltpu.VMEM((variables, latent), BF16),
            square,
            pltpu.VMEM((1, points), jnp.int32),
            pltpu.VMEM((1, points), jnp.int32),
            square,
            pltpu.VMEM((mesh_links.shape[3], 1, nodes), jnp.int32),
            cube,
            cube,
            cube,
            square,
            pltpu.VMEM((variables, latent), BF16),
            pltpu.VMEM((points, latent), BF16),
            pltpu.VMEM((points, latent), BF16),
            pltpu.VMEM((n_lon, 2 * nodes, latent // 2), BF16),
            pltpu.VMEM((n_lon - 1, 2 * nodes, latent // 2), BF16),
            pltpu.VMEM((layers, 9, 2 * nodes, latent // 2), BF16),
            pltpu.VMEM((n_lon, rows, variables), BF16),
            pltpu.VMEM((variables, points), jnp.float32),
            pltpu.SemaphoreType.DMA((12,)),
            pltpu.SemaphoreType.DMA((n_lon - 1,)),
            pltpu.SemaphoreType.DMA((n_lon - 1,)),
            pltpu.SemaphoreType.DMA((layers, 9)),
            pltpu.SemaphoreType.DMA((layers, 9)),
            pltpu.SemaphoreType.DMA((n_lon - 1,)),
            pltpu.SemaphoreType.DMA((n_lon - 1,)),
        ],
        compiler_params=pltpu.CompilerParams(
            collective_id=0, has_side_effects=True, vmem_limit_bytes=LIMIT * 1024 * 1024
        ),
    )(
        jnp.swapaxes(grid_input.reshape(points, variables), 0, 1),
        w_grid,
        w_send,
        to_sector.reshape(1, points),
        to_node.reshape(1, points),
        w_node,
        jnp.transpose(mesh_links, (0, 3, 1, 2)).reshape(-1, 1, nodes),
        w_source,
        w_target,
        w_update,
        w_decode,
        jnp.swapaxes(w_output, 0, 1),
    )
    return (jnp.swapaxes(result, 0, 1).reshape(1, 1, points, variables), state.reshape(1, 1, nodes, latent))


def solution(mesh):
    placed = (
        P("lat", "lon", None, None),
        P(),
        P(),
        P("lat", "lon", None, None),
        P("lat", "lon", None),
        P(),
        P("lat", "lon", None, None),
        P(),
        P(),
        P(),
        P(),
        P(),
    )
    return jax.shard_map(
        body,
        mesh=mesh,
        in_specs=placed,
        out_specs=(P("lat", "lon", None, None), P("lat", "lon", None, None)),
        check_vma=False,
    )
```

time: 43.9 us -> 30.5 us (0.69)
  local copies, waits for them, and re-layouts: 12.4 us -> 2.37 us
  Pallas kernels: 30.3 us -> 27.3 us
    unnamed x27 -> x4, local copies, waits for them, and re-layouts: 12.4 us -> 2.37 us
    pallas_call x1, Pallas kernels: 30.3 us -> 27.3 us  [body(): pl.pallas_call(functools.partial(kernel, n_lat, n_lon, RELAYED, chunk), o...]
where the time goes in v2:
time: 30.5 us; the launch traced here: 30.3 us
  Pallas kernels  27.3 us (90%)
  local copies, waits for them, and re-layouts  2.37 us (8%)
  between operations  0.65 us (2%)
    pallas_call x1, Pallas kernels, body(): pl.pallas_call(functools.partial(kernel, n_lat, n_lon, RELAYED, chunk), o...  27.3 us
    unnamed x4, local copies, waits for them, and re-layouts  2.37 us

profile of v2, /device:TPU:9, one launch (start us, length us, event | category | flops | bytes accessed | tf_op | source)
XLA Modules:
  0.0 30.3 jit_solution(17193445664296071639)
XLA Ops:
  0.6 27.3 %shard_map.131 = (bf16[227,720]{1,0:T(8,128)(2,1)}, bf16[40,512]{1,0:T(8,128)(2,1)}) custom-call(bf16[227,720]{1,0:T(8,128)(2,1)} %bitcast.14, bf16[227,512]{1,0:T(8,128)(2,1)} %wg_hbm.1, bf16[512,512]{1,0:T(8,128)(2,1)} %ws_hbm.1, s32[1,720]{1,0:T(1,128)} %bitcast.17, s32[1,720]{1,0:T(1,128)} %bitcast.18, bf16[512,512]{1,0:T(8,128)(2,1)} %wn_hbm.1, ...), custom_call_target="tpu_custom_call" | custom-call | tf_op jit(solution)/shard_map/pallas_call | solution.py:372
  27.9 0.0 copy-start
  27.9 1.7 %copy.16 = bf16[1,1,720,227]{2,3,1,0:T(8,128)(2,1)} copy(bf16[1,1,720,227]{2,3,1,0:T(8,128)(2,1)} %bitcast.13) | data formatting | bytes 653760
  29.7 0.0 copy-done
  29.7 0.6 %copy.17 = bf16[1,1,40,512]{3,2,1,0:T(8,128)(2,1)} copy(bf16[1,1,40,512]{3,2,1,0:T(8,128)(2,1)S(1)} %bitcast.16) | data formatting | bytes 81920
Async XLA Ops:
  27.9 1.8 %copy-start = (bf16[40,512]{1,0:T(8,128)(2,1)S(1)}, bf16[40,512]{1,0:T(8,128)(2,1)}, u32[]{:S(2)}) copy-start(bf16[40,512]{1,0:T(8,128)(2,1)} %get-tuple-element.5) | copy-start | bytes 122884

commit v3 on v2

--- a/solution.py
+++ b/solution.py
@@ -9,7 +9,7 @@
 
 MESH = pl.DeviceIdType.MESH
 BF16 = jnp.bfloat16
-RELAYED = ()
+RELAYED = (1,)
 LIMIT = 56
 
 
@@ -372,8 +372,8 @@
     result, state = pl.pallas_call(
         functools.partial(kernel, n_lat, n_lon, RELAYED, chunk),
         out_shape=(
-            jax.ShapeDtypeStruct((variables, points), BF16),
-            jax.ShapeDtypeStruct((nodes, latent), BF16),
+            pltpu.VMEM((variables, points), BF16),
+            pltpu.VMEM((nodes, latent), BF16),
         ),
         in_specs=[hbm] * 12,
         out_specs=(vmem, vmem),

time: 30.5 us -> 26.7 us (0.88)
  Pallas kernels: 27.3 us -> 24.5 us
  local copies, waits for them, and re-layouts: 2.37 us -> 1.35 us
    pallas_call x1, Pallas kernels: 27.3 us -> 24.5 us  [body(): pl.pallas_call(functools.partial(kernel, n_lat, n_lon, RELAYED, chunk), o...]
    unnamed x4 -> x2, local copies, waits for them, and re-layouts: 2.37 us -> 1.35 us
where the time goes in v3:
time: 26.7 us; the launch traced here: 26.5 us
  Pallas kernels  24.5 us (92%)
  local copies, waits for them, and re-layouts  1.35 us (5%)
  between operations  0.64 us (2%)
    pallas_call x1, Pallas kernels, body(): pl.pallas_call(functools.partial(kernel, n_lat, n_lon, RELAYED, chunk), o...  24.5 us
    unnamed x2, local copies, waits for them, and re-layouts  1.35 us

profile of v3, /device:TPU:9, one launch (start us, length us, event | category | flops | bytes accessed | tf_op | source)
XLA Modules:
  0.0 26.5 jit_solution(14723347495564929146)
XLA Ops:
  0.6 24.5 %shard_map.131 = (bf16[227,720]{1,0:T(8,128)(2,1)S(1)}, bf16[40,512]{1,0:T(8,128)(2,1)S(1)}) custom-call(bf16[227,720]{1,0:T(8,128)(2,1)} %bitcast.15, bf16[227,512]{1,0:T(8,128)(2,1)} %wg_hbm.1, bf16[512,512]{1,0:T(8,128)(2,1)} %ws_hbm.1, s32[1,720]{1,0:T(1,128)} %bitcast.17, s32[1,720]{1,0:T(1,128)} %bitcast.18, bf16[512,512]{1,0:T(8,128)(2,1)} %wn_hbm.1, ...), custom_call_target="tpu_custom_call" | custom-call | tf_op jit(solution)/shard_map/pallas_call | solution.py:372
  25.2 0.7 %copy.16 = bf16[1,1,720,227]{2,3,1,0:T(8,128)(2,1)} copy(bf16[1,1,720,227]{2,3,1,0:T(8,128)(2,1)S(1)} %bitcast.13) | data formatting | bytes 653760
  25.9 0.6 %copy.17 = bf16[1,1,40,512]{3,2,1,0:T(8,128)(2,1)} copy(bf16[1,1,40,512]{3,2,1,0:T(8,128)(2,1)S(1)} %bitcast.14) | data formatting | bytes 81920

commit v4 on v3

--- a/solution.py
+++ b/solution.py
@@ -196,9 +196,14 @@
     lon_step = cell % 3 - 1
     column = jnp.where(lon_step == 0, 0, jnp.where(lon_step == side, 1, 2))
     links = links - cell * nodes + ((cell // 3) * 3 + column) * (2 * nodes)
-    slots = lax.broadcasted_iota(jnp.int32, (degree * nodes, 18 * nodes), 1)
-    wanted_low = jnp.where(slots == links, 1.0, 0.0).astype(BF16)
-    wanted_high = jnp.where(slots == links + nodes, 1.0, 0.0).astype(BF16)
+    slots = lax.broadcasted_iota(jnp.int32, (degree * nodes, 6 * nodes), 1)
+    wanted = [
+        [
+            jnp.where(slots == links + (shift - row * 6) * nodes, 1.0, 0.0).astype(BF16)
+            for shift in (0, 1)
+        ]
+        for row in range(3)
+    ]
     answered = sector_of[...] * rows + node_of[...]
     fetching = jnp.where(
         lax.broadcasted_iota(jnp.int32, (n_lon * rows, points), 0) == answered, 1.0, 0.0
@@ -265,22 +270,29 @@
             for column in relayed:
                 forward(layer, 2, column).start()
 
+        def pick(row):
+            senders = table[layer, 3 * row : 3 * row + 3].reshape(6 * nodes, half)
+            return [matmul(which, senders) for which in wanted[row]]
+
         for column in (1, 2):
             halo(layer, 0, column).wait_recv()
+        picks = [pick(1)]
 
         @pl.when(has_low)
         def _():
             for column in (2, 1):
                 halo(layer, 1, column).wait_recv()
 
+        picks.append(pick(0))
+
         @pl.when(has_high)
         def _():
             for column in (2, 1):
                 halo(layer, -1, column).wait_recv()
 
-        senders = table[layer].reshape(18 * nodes, half)
+        picks.append(pick(2))
         picked = jnp.concatenate(
-            [matmul(wanted_low, senders), matmul(wanted_high, senders)], axis=1
+            [picks[0][i] + picks[1][i] + picks[2][i] for i in (0, 1)], axis=1
         )
         summed = silu(picked[0:nodes] + toward)
         for k in range(1, degree):

time: 26.7 us -> 26.6 us (level)
  no operation moved by 1% of the time
where the time goes in v4:
time: 26.6 us; the launch traced here: 26.5 us
  Pallas kernels  24.5 us (92%)
  local copies, waits for them, and re-layouts  1.35 us (5%)
  between operations  0.64 us (2%)
    pallas_call x1, Pallas kernels, body(): pl.pallas_call(functools.partial(kernel, n_lat, n_lon, RELAYED, chunk), o...  24.5 us
    unnamed x2, local copies, waits for them, and re-layouts  1.35 us

profile of v4, /device:TPU:9, one launch (start us, length us, event | category | flops | bytes accessed | tf_op | source)
XLA Modules:
  0.0 26.5 jit_solution(7687457927171090586)
XLA Ops:
  0.6 24.5 %shard_map.131 = (bf16[227,720]{1,0:T(8,128)(2,1)S(1)}, bf16[40,512]{1,0:T(8,128)(2,1)S(1)}) custom-call(bf16[227,720]{1,0:T(8,128)(2,1)} %bitcast.15, bf16[227,512]{1,0:T(8,128)(2,1)} %wg_hbm.1, bf16[512,512]{1,0:T(8,128)(2,1)} %ws_hbm.1, s32[1,720]{1,0:T(1,128)} %bitcast.17, s32[1,720]{1,0:T(1,128)} %bitcast.18, bf16[512,512]{1,0:T(8,128)(2,1)} %wn_hbm.1, ...), custom_call_target="tpu_custom_call" | custom-call | tf_op jit(solution)/shard_map/pallas_call | solution.py:384
  25.1 0.7 %copy.16 = bf16[1,1,720,227]{2,3,1,0:T(8,128)(2,1)} copy(bf16[1,1,720,227]{2,3,1,0:T(8,128)(2,1)S(1)} %bitcast.13) | data formatting | bytes 653760
  25.9 0.6 %copy.17 = bf16[1,1,40,512]{3,2,1,0:T(8,128)(2,1)} copy(bf16[1,1,40,512]{3,2,1,0:T(8,128)(2,1)S(1)} %bitcast.14) | data formatting | bytes 81920
